TPU v7x, 512 devices: a whole 4x8x8 slice. The times are simulated.
512 devices in a mesh: ctx: 8 (over x, core), vocab: 64 (over z, y).
Axes of the slice: x: 4, y: 8, z: 8, core: 2. Of those that a mesh axis runs over, the one named last changes fastest.
Arguments:
- hidden: bfloat16 [1024, 8192], P('ctx')
- head: bfloat16 [8192, 65536], P('ctx', 'vocab')
- targets: int32 [1024], P('ctx'), may hold values from 0 to 65535
- loss_mask: int32 [1024], P('ctx'), may hold values 0 or 1
- example_ids: int32 [1024], P('ctx'), may hold values from 0 to 1, never falling along the last dimension, each value on 1 to 768 neighbouring positions
- down_input: bfloat16 [1024, 28672], P('ctx', 'vocab'), may hold values from -6 to 6
- proj_hidden: bfloat16 [8192, 64], P('ctx'), may hold values from -0.0625 to 0.0625
- proj_vocab: bfloat16 [65536, 64], P('vocab'), may hold values from -6 to 6
- proj_grad: bfloat16 [8192, 64], P('ctx'), may hold values from -1.5 to 1.5
- proj_act: bfloat16 [28672, 64], P('vocab'), may hold values from -0.03125 to 0.03125
Outputs:
- head_features: float32 [2, 4096], replicated
- down_features: float32 [2, 4096], replicated
Inputs may be any that keep to these rules, and one draw needn't show every extreme that they name: `example_ids`: example numbers never fall along the tokens; each example has 1 to 768 tokens.
All inputs are finite; a program needn't handle non-finite values. No bound on the sum of `loss_mask` on one device may be relied on, other than what follows from the above.
Results may differ from a plain program's by a relative error of at most 0.0015.
Values may be sent and summed in bfloat16 or wider, within the bound.
A program may use at most 64 MiB of HBM per device.

v0:
```python
import jax
import jax.numpy as jnp
from jax import lax
from jax.sharding import PartitionSpec as P

EXAMPLES = 2


def local(
    hidden,
    head,
    targets,
    loss_mask,
    example_ids,
    down_input,
    proj_hidden,
    proj_vocab,
    proj_grad,
    proj_act,
):
    tok_rows = hidden.shape[0]
    voc_cols = head.shape[1]
    full_basis = lax.all_gather(proj_hidden, "ctx", axis=0, tiled=True)
    hidden_proj = jnp.dot(hidden, full_basis, preferred_element_type=jnp.float32)
    act_part = jnp.dot(down_input, proj_act, preferred_element_type=jnp.float32)
    spread = lax.all_to_all(hidden, "ctx", split_axis=1, concat_axis=0, tiled=True)
    logits = lax.psum_scatter(
        jnp.dot(spread, head, preferred_element_type=jnp.float32),
        "ctx",
        scatter_dimension=0,
        tiled=True,
    )
    local_top = jnp.max(logits, axis=1)
    row_top = lax.pmax(local_top, "vocab")
    shifted = jnp.exp(logits - row_top[:, None])
    row_total = lax.psum(jnp.sum(shifted, axis=1), "vocab")
    column_ids = jnp.arange(voc_cols, dtype=jnp.int32) + lax.axis_index("vocab") * voc_cols
    onehot = (targets[:, None] == column_ids[None, :]).astype(jnp.float32)
    weights_mask = loss_mask.astype(jnp.float32)[:, None]
    token_grad = (weights_mask * (shifted / row_total[:, None] - onehot)).astype(jnp.bfloat16)
    grad_part = jnp.dot(token_grad, proj_vocab, preferred_element_type=jnp.float32)
    act_proj, grad_proj = lax.psum((act_part, grad_part), "vocab")
    every_grad = lax.all_gather(token_grad, "ctx", axis=0, tiled=True)
    backward = lax.dot_general(
        every_grad, head, (((1,), (1,)), ((), ())), preferred_element_type=jnp.float32
    )
    partial_value = jnp.dot(
        backward, proj_grad.astype(jnp.float32), precision=lax.Precision.HIGHEST
    )
    summed = lax.psum(partial_value, ("ctx", "vocab"))
    down_proj = lax.dynamic_slice_in_dim(summed, lax.axis_index("ctx") * tok_rows, tok_rows, 0)
    rank_size = hidden_proj.shape[1]
    membership = (example_ids[None, :] == jnp.arange(EXAMPLES, dtype=jnp.int32)[:, None]).astype(
        jnp.float32
    )
    factor = (tok_rows * lax.axis_size("ctx")) ** (-0.5)
    outer_head = (hidden_proj[:, :, None] * grad_proj[:, None, :]).reshape(
        tok_rows, rank_size * rank_size
    )
    outer_down = (act_proj[:, :, None] * down_proj[:, None, :]).reshape(
        tok_rows, rank_size * rank_size
    )
    head_local = factor * jnp.dot(membership, outer_head, precision=lax.Precision.HIGHEST)
    down_local = factor * jnp.dot(membership, outer_down, precision=lax.Precision.HIGHEST)
    head_features, down_features = lax.psum((head_local, down_local), "ctx")
    return (head_features, down_features)


def solution(mesh):
    return jax.shard_map(
        local,
        mesh=mesh,
        in_specs=(
            P("ctx", None),
            P("ctx", "vocab"),
            P("ctx"),
            P("ctx"),
            P("ctx"),
            P("ctx", "vocab"),
            P("ctx", None),
            P("vocab", None),
            P("ctx", None),
            P("vocab", None),
        ),
        out_specs=(P(), P()),
        check_vma=False,
    )
```

profile of v0, /device:TPU:1, one launch (start us, length us, event | category | flops | bytes accessed | tf_op | source)
XLA Modules:
  0.0 911.8 jit_solution(9264351563213870543)
XLA Ops:
  7.2 4.2 copy.16
  11.4 37.7 %all_to_all.19 = bf16[128,8,1024]{0,2,1:T(8,128)(2,1)} all-to-all(bf16[128,8,1024]{0,2,1:T(8,128)(2,1)} %bitcast.22), channel_id=1, replica_groups=mesh['ctx'=8,'vocab'=64] {'ctx'}, dimensions={1} | all-to-all | bytes 4194304 | tf_op jit(solution)/shard_map/all_to_all | solution.py:26
  49.1 3.9 copy.17
  53.0 5.9 fusion.4
  59.7 38.1 %reduce-scatter.2.cloned.1.call-done = f32[128,1024]{1,0:T(8,128)} async-done(((f32[1024,1024]{1,0:T(8,128)}), f32[128,1024]{1,0:T(8,128)}) %reduce-scatter.2.cloned.1.call-update) | async-done | bytes 524304 | tf_op jit(solution)/shard_map/reduce_scatter | solution.py:27
  97.8 1.2 reduce_max.9
  99.0 115.9 %pmax.7 = f32[128]{0:T(128)S(1)} all-reduce(f32[128]{0:T(128)S(1)} %reduce_max.9), channel_id=1, replica_groups=mesh['ctx'=8,'vocab'=64] {'vocab'}, use_global_device_ids=true, to_apply=%region_2.0 | all-reduce | flops 128 | bytes 1024 | tf_op jit(solution)/shard_map/pmax | solution.py:34
  214.9 1.3 fusion
  216.1 110.8 %psum.42 = f32[128]{0:T(128)S(1)} all-reduce(f32[128]{0:T(128)S(1)} %fusion), channel_id=1, replica_groups=mesh['ctx'=8,'vocab'=64] {'vocab'}, use_global_device_ids=true, to_apply=%region_4.0 | all-reduce | flops 128 | bytes 1024 | tf_op jit(solution)/shard_map/psum | solution.py:36
  327.0 2.0 multiply_convert_fusion
  329.1 0.8 fusion.8
  329.8 2.7 fusion.3
  332.5 77.1 %all-gather.5.cloned.1.call-done = bf16[1024,1024]{1,0:T(8,128)(2,1)} async-done(((bf16[128,1024]{1,0:T(8,128)(2,1)}), bf16[1024,1024]{1,0:T(8,128)(2,1)}) %all-gather.5.cloned.1.call-update) | async-done | bytes 2097168 | tf_op jit(solution)/shard_map/all_gather | solution.py:43
  409.7 4.0 fusion.6
  413.7 3.0 fusion.7
  416.8 0.8 fusion.5
  417.7 266.6 %all-reduce.6.cloned.1.call-done = f32[1024,64]{0,1:T(8,128)} async-done(((f32[1024,64]{0,1:T(8,128)}), f32[1024,64]{0,1:T(8,128)}) %all-reduce.6.cloned.1.call-update) | async-done | bytes 262160 | tf_op jit(solution)/shard_map/psum | solution.py:50
  685.1 144.7 %all-reduce.8.cloned.1.call-done = (f32[128,64]{0,1:T(8,128)}, f32[128,64]{0,1:T(8,128)}) async-done(((f32[128,64]{0,1:T(8,128)}, f32[128,64]{0,1:T(8,128)}), (f32[128,64]{0,1:T(8,128)}, f32[128,64]{0,1:T(8,128)})) %all-reduce.8.cloned.1.call-update) | async-done | bytes 65552 | tf_op jit(solution)/shard_map/psum | solution.py:42
  829.8 1.4 broadcast_multiply_fusion
  831.2 1.7 convolution_multiply_fusion
  832.9 1.7 convolution_multiply_fusion.1
  834.6 67.6 %all-reduce.10.cloned.1.call-done = (f32[2,4096]{1,0:T(2,128)}, f32[2,4096]{1,0:T(2,128)}) async-done(((f32[2,4096]{1,0:T(2,128)}, f32[2,4096]{1,0:T(2,128)}), (f32[2,4096]{1,0:T(2,128)}, f32[2,4096]{1,0:T(2,128)})) %all-reduce.10.cloned.1.call-update) | async-done | bytes 65552 | tf_op jit(solution)/shard_map/psum | solution.py:65
  902.2 1.4 copy.23
  903.6 1.4 copy.24
  (34 shorter events, 1.8 us)
Async XLA Ops:
  7.2 45.8 %copy-start = (bf16[1024,1024]{1,0:T(8,128)(2,1)S(1)}, bf16[1024,1024]{1,0:T(8,128)(2,1)}, u32[]{:S(2)}) copy-start(bf16[1024,1024]{1,0:T(8,128)(2,1)} %param.11) | copy-start | bytes 6291460
  7.2 90.6 %reduce-scatter.2.cloned.1.call-start = ((), (), s32[]{:S(2)}) async-start(), calls=%async_computation.3 | async-start | bytes 4718592 | tf_op jit(solution)/shard_map/reduce_scatter | solution.py:27
  58.9 0.9 copy-start.8
  58.9 268.1 %copy-start.7 = (s32[128]{0:T(128)S(1)}, s32[128]{0:T(128)}, u32[]{:S(2)}) copy-start(s32[128]{0:T(128)} %param.12) | copy-start | bytes 1540
  58.9 270.2 %copy-start.4 = (bf16[128,448]{0,1:T(8,128)(2,1)S(1)}, bf16[128,448]{0,1:T(8,128)(2,1)}, u32[]{:S(2)}) copy-start(bf16[128,448]{0,1:T(8,128)(2,1)} %param.15) | copy-start | bytes 344068
  58.9 270.2 %copy-start.5 = (bf16[448,64]{0,1:T(8,128)(2,1)S(1)}, bf16[448,64]{0,1:T(8,128)(2,1)}, u32[]{:S(2)}) copy-start(bf16[448,64]{0,1:T(8,128)(2,1)} %param.19) | copy-start | bytes 172036
  58.9 270.9 %all-gather.3.cloned.1.call-start = ((), (), s32[]{:S(2)}) async-start(), calls=%async_computation.2 | async-start | bytes 1179648 | tf_op jit(solution)/shard_map/all_gather | solution.py:23
  59.7 350.0 %all-gather.5.cloned.1.call-start = ((), (), s32[]{:S(2)}) async-start(), calls=%async_computation.4 | async-start | bytes 2359296 | tf_op jit(solution)/shard_map/all_gather | solution.py:43
  329.0 355.3 %all-reduce.6.cloned.1.call-start = ((), (), s32[]{:S(2)}) async-start(), calls=%async_computation.5 | async-start | bytes 524288 | tf_op jit(solution)/shard_map/psum | solution.py:50
  332.5 81.1 %copy-start.2 = (bf16[1024,64]{0,1:T(8,128)(2,1)S(1)}, bf16[1024,64]{0,1:T(8,128)(2,1)}, u32[]{:S(2)}) copy-start(bf16[1024,64]{0,1:T(8,128)(2,1)} %param.18) | copy-start | bytes 393220
  413.6 3.1 copy-start.1
  413.6 3.1 copy-start.3
  416.7 413.0 %all-reduce.8.cloned.1.call-start = ((), (), s32[]{:S(2)}) async-start(), calls=%async_computation.6 | async-start | bytes 131072 | tf_op jit(solution)/shard_map/psum | solution.py:42
  417.6 484.6 %all-reduce.10.cloned.1.call-start = ((), (), s32[]{:S(2)}) async-start(), calls=%async_computation.7 | async-start | bytes 131072 | tf_op jit(solution)/shard_map/psum | solution.py:65
  829.8 1.4 copy-start.6
Sparse Core Ops, SparseCore 0:
  59.0 38.7 reduce-scatter.1
  100.0 30.5 all-gather.2
  329.1 80.5 all-gather.4
  416.8 267.4 all-reduce.5
  688.5 141.2 all-reduce.7
  834.7 67.4 all-reduce.9
where the time goes:
time: 913 us; the launch traced here: 912 us
  waiting for transfers between devices  595 us (65%)
  blocking collectives  264 us (29%)
  matrix products  20.6 us (2%)
  between operations  14.3 us (2%)
  local copies, waits for them, and re-layouts  11.7 us (1%)
    psum x1, waiting for transfers between devices, local(): summed = lax.psum(partial_value, ('ctx', 'vocab'))  267 us
    psum x1, waiting for transfers between devices, local(): act_proj, grad_proj = lax.psum((act_part, grad_part), 'vocab')  145 us
    pmax x1, blocking collectives, local(): row_top = lax.pmax(local_top, 'vocab')  116 us
    psum x1, blocking collectives, local(): row_total = lax.psum(jnp.sum(shifted, axis=1), 'vocab')  111 us
    all_gather x1, waiting for transfers between devices, local(): every_grad = lax.all_gather(token_grad, 'ctx', axis=0, tiled=True)  77.1 us
    psum x1, waiting for transfers between devices, local(): head_features, down_features = lax.psum((head_local, down_local), 'ctx')  67.6 us
    reduce_scatter x1, waiting for transfers between devices, local(): lax.psum_scatter(jnp.dot(spread, head, preferred_element_type=jnp.float32...  38.1 us
    all_to_all x1, blocking collectives, local(): lax.all_to_all(hidden, 'ctx', split_axis=1, concat_axis=0, tiled=True)  37.7 us
  transfers between devices with their start and end apart: 6, of which 5 were waited for; matrix products, arithmetic and copies ran while one was open for 1% of the time, Pallas kernels for 0%

commit v1 on v0

v1 whole, which is shorter than its diff:
```python
import functools

import jax
import jax.numpy as jnp
from jax import lax
from jax.experimental import pallas as pl
from jax.experimental.pallas import tpu as pltpu
from jax.sharding import PartitionSpec as P

MESH = pl.DeviceIdType.MESH
NX, NC, NY, NZ = 4, 2, 8, 8
EXAMPLES = 2
COPIES = 67
NT = (((1,), (1,)), ((), ()))
TN = (((0,), (0,)), ((), ()))
F32, BF16 = jnp.float32, jnp.bfloat16


def kernel(
    hidden, head, ids, down_input, ph, pv, pg, pa,
    out,
    heads, hid, fwd, pgs, phs, gpart, grecv, gfull, hps, hrecv,
    part, recv_a, recv_b, w, vy, ry, vz, rz, mz, az, my, ay, feat, rc, mc, fa,
    lsem, ssem, rsem,
):
    i, j = lax.axis_index("ctx"), lax.axis_index("vocab")
    x, c = i // NC, i % NC
    z, y = j // NY, j % NY

    def peer(dx=0, dc=0, dy=0, dz=0):
        return (
            ((x + dx) % NX) * NC + (c + dc) % NC,
            ((z + dz) % NZ) * NY + (y + dy) % NY,
        )

    ctx_peers = [(dx, dc) for dx in range(NX) for dc in range(NC) if dx or dc]
    started = []

    def send(src, dst, to):
        k = len(started)
        copy = pltpu.make_async_remote_copy(
            src_ref=src, dst_ref=dst, send_sem=ssem.at[k], recv_sem=rsem.at[k],
            device_id=to, device_id_type=MESH,
        )
        copy.start()
        started.append(copy)
        return copy

    def dot(a, b, dims=NT):
        return lax.dot_general(a, b, dims, preferred_element_type=F32)

    dm = heads.shape[1]
    wide = NC * dm
    vc = heads.shape[2]
    half = vc // 2
    rows = hid.shape[1]
    low = lax.broadcasted_iota(jnp.int32, (1, 128), 1) < 64

    def columns_of(chip):
        return pl.ds(pl.multiple_of(chip * wide, 128), wide)

    own_head = pltpu.make_async_copy(head, heads.at[c], lsem.at[0])
    own_head.start()
    own_hid = pltpu.make_async_copy(hidden.at[:, columns_of(x)], hid.at[x], lsem.at[1])
    own_hid.start()

    barrier = pltpu.get_barrier_semaphore()
    for dx, dc in ctx_peers:
        pl.semaphore_signal(barrier, inc=1, device_id=peer(dx, dc), device_id_type=MESH)
    for d in range(1, NY):
        pl.semaphore_signal(barrier, inc=1, device_id=peer(dy=d), device_id_type=MESH)
    for d in range(1, NZ):
        pl.semaphore_signal(barrier, inc=1, device_id=peer(dz=d), device_id_type=MESH)
    pl.semaphore_wait(barrier, len(ctx_peers) + NY - 1 + NZ - 1)

    right, left = peer(dx=1), peer(dx=NX - 1)
    sibling = peer(dc=1)
    xr, xl, xo = (x + 1) % NX, (x + NX - 1) % NX, (x + 2) % NX

    hr = rows // 2
    to_opp_r = send(hidden.at[pl.ds(0, hr), columns_of(xo)], fwd.at[0], right)
    to_opp_l = send(hidden.at[pl.ds(hr, hr), columns_of(xo)], fwd.at[1], left)
    head_copy = send(head, heads.at[c], sibling)
    pg_copy = send(pg, pgs.at[c], sibling)
    ph_copy = send(ph, phs.at[c], sibling)
    hid_r = send(hidden.at[:, columns_of(xr)], hid.at[x], right)
    hid_l = send(hidden.at[:, columns_of(xl)], hid.at[x], left)

    pgs[c] = pg[...]
    phs[c] = ph[...]

    act_t = dot(pa[...], down_input[...], (((1,), (0,)), ((), ())))
    act = jnp.concatenate([act_t, act_t], axis=0).T

    to_opp_r.wait_recv()
    fwd_r = send(fwd.at[0], hid.at[xl, pl.ds(0, hr)], right)
    to_opp_l.wait_recv()
    fwd_l = send(fwd.at[1], hid.at[xr, pl.ds(hr, hr)], left)

    own_head.wait()
    head_copy.wait_recv()
    pg_copy.wait_recv()
    quarter = vc // NX
    for q in range(NX):
        cols = pl.ds(q * quarter, quarter)
        gpart[q] = sum(
            dot(pgs[k], heads[k, :, cols], (((1,), (0,)), ((), ()))) for k in range(NC)
        )
    hr64 = gpart.shape[1] // NC
    mine = pl.ds(pl.multiple_of(c * hr64, 8), hr64)
    g_sum = [
        send(gpart.at[(x + d) % NX, mine], grecv.at[d - 1], peer(dx=d)) for d in range(1, NX)
    ]
    ph_copy.wait_recv()

    def logits(chip, slot, h):
        cols = pl.ds(h * half, half)
        part[slot, h] = sum(
            dot(
                hid[chip, :, k * dm : (k + 1) * dm], heads[k, :, cols],
                (((1,), (0,)), ((), ())),
            )
            for k in range(NC)
        )

    def project(chip):
        hp = sum(dot(hid[chip, :, k * dm : (k + 1) * dm], phs[k]) for k in range(NC))
        hps[chip] = jnp.concatenate([hp, hp], axis=1)

    own_hid.wait()
    for h in range(2):
        logits(x, 3, h)
    project(x)

    for copy in g_sum:
        copy.wait_recv()
    gfull[x, mine] = gpart[x, mine] + grecv[0] + grecv[1] + grecv[2]
    g_all = [
        send(gfull.at[x, mine], gfull.at[x, mine], peer(dx=d)) for d in range(1, NX)
    ]

    owner = NZ * y + z
    group = pl.ds(pl.multiple_of((owner // 4) * 8, 8), 8)

    hid_r.wait_recv()
    logits(xl, 2, 0)
    s_l0 = send(part.at[2, 0], recv_b.at[1, 0], left)
    logits(xl, 2, 1)
    hid_l.wait_recv()
    logits(xr, 1, 1)
    s_r1 = send(part.at[1, 1], recv_b.at[0, 1], right)
    logits(xr, 1, 0)
    fwd_r.wait_recv()
    fwd_l.wait_recv()
    logits(xo, 0, 0)
    a_r = send(part.at[0, 0], recv_a.at[0], right)
    logits(xo, 0, 1)
    a_l = send(part.at[0, 1], recv_a.at[1], left)

    for chip in (xl, xr, xo):
        project(chip)
    hp_sum = [
        send(hps.at[(x + d) % NX, group], hrecv.at[d - 1], peer(dx=d)) for d in range(1, NX)
    ]

    a_r.wait_recv()
    part[1, 0] = part[1, 0] + recv_a[0]
    s_r0 = send(part.at[1, 0], recv_b.at[0, 0], right)
    a_l.wait_recv()
    part[2, 1] = part[2, 1] + recv_a[1]
    s_l1 = send(part.at[2, 1], recv_b.at[1, 1], left)

    for copy in g_all:
        copy.wait_recv()
    g_sib = send(gfull.at[:, mine], gfull.at[:, mine], sibling)
    g_sib.wait_recv()
    for q in range(NX):
        cols = pl.ds(q * quarter, quarter)
        g = gfull[q]
        high = g.astype(BF16)
        w[0:64, cols] = pv[:, cols]
        w[64:128, cols] = high
        w[128:192, cols] = jnp.zeros_like(high)
        w[192:256, cols] = (g - high.astype(F32)).astype(BF16)

    id_cols = [jnp.broadcast_to(ids[k : k + 1, :], (rows, rows)).T for k in range(3)]
    target = id_cols[0][:, 0:1]

    for copy in (s_l0, s_r1, s_r0, s_l1):
        copy.wait_recv()
    vals = [part[3, h] + recv_b[0, h] + recv_b[1, h] for h in range(2)]
    top = jnp.maximum(
        jnp.max(vals[0], axis=1, keepdims=True), jnp.max(vals[1], axis=1, keepdims=True)
    )
    total = jnp.zeros_like(top)
    acc = jnp.zeros((3 * rows, 256), F32)
    for h in range(2):
        e = jnp.exp(vals[h] - top)
        total = total + jnp.sum(e, axis=1, keepdims=True)
        e_high = e.astype(BF16)
        e_low = (e - e_high.astype(F32)).astype(BF16)
        ids_here = lax.broadcasted_iota(jnp.int32, (rows, half), 1) + (j * vc + h * half)
        onehot = jnp.where(ids_here == target, 1.0, 0.0).astype(BF16)
        lhs = jnp.concatenate([e_high, e_low, onehot], axis=0)
        acc = acc + dot(lhs, w[:, h * half : (h + 1) * half])
    both = acc[:, 0:128] + acc[:, 128:256]

    per = 4
    vy[pl.ds(0, rows, stride=per), :] = both[0:rows] + both[rows : 2 * rows]
    vy[pl.ds(1, rows, stride=per), :] = both[2 * rows :]
    vy[pl.ds(2, rows, stride=per), :] = jnp.where(low, act, total)
    vy[pl.ds(3, rows, stride=per), :] = jnp.broadcast_to(top, (rows, 128))

    chunk = vy.shape[0] // NY
    got = [
        send(vy.at[pl.ds(pl.multiple_of(((y + d) % NY) * chunk, 8), chunk)], ry.at[d], peer(dy=d))
        for d in range(1, NY)
    ]
    ry[0] = vy[pl.ds(pl.multiple_of(y * chunk, 8), chunk), :]
    for copy in got:
        copy.wait_recv()
    n = chunk // per
    tops = [ry[d, pl.ds(3, n, stride=per), :] for d in range(NY)]
    best = functools.reduce(jnp.maximum, tops)
    scale = [jnp.exp(t - best) for t in tops]
    mixed = [ry[d, pl.ds(2, n, stride=per), :] for d in range(NY)]
    vz[pl.ds(0, n, stride=per), :] = sum(
        scale[d] * ry[d, pl.ds(0, n, stride=per), :] for d in range(NY)
    )
    vz[pl.ds(1, n, stride=per), :] = sum(ry[d, pl.ds(1, n, stride=per), :] for d in range(NY))
    vz[pl.ds(2, n, stride=per), :] = sum(
        jnp.where(low, mixed[d], mixed[d] * scale[d]) for d in range(NY)
    )
    vz[pl.ds(3, n, stride=per), :] = best

    got = [
        send(vz.at[pl.ds(pl.multiple_of(((z + d) % NZ) * 8, 8), 8)], rz.at[pl.ds(8 * d, 8)], peer(dz=d))
        for d in range(1, NZ)
    ]
    rz[0:8, :] = vz[pl.ds(pl.multiple_of(z * 8, 8), 8), :]
    for copy in hp_sum:
        copy.wait_recv()
    hp_rows = hps[x, group, :] + hrecv[0] + hrecv[1] + hrecv[2]
    row_ids = lax.broadcasted_iota(jnp.int32, (8, 1), 0)
    for copy in got:
        copy.wait_recv()
    mz[...] = jnp.zeros_like(mz)
    for t in range(2):
        at = [rz[pl.ds(4 * t + k, NZ, stride=8), :] for k in range(4)]
        best = jnp.max(at[3], axis=0, keepdims=True)
        scale = jnp.exp(at[3] - best)
        soft = jnp.sum(scale * at[0], axis=0, keepdims=True)
        hot = jnp.sum(at[1], axis=0, keepdims=True)
        mix = jnp.sum(jnp.where(low, at[2], at[2] * scale), axis=0, keepdims=True)
        denominator = jnp.where(low, pltpu.roll(mix, 64, 1), mix)
        hp = jnp.sum(
            jnp.where(row_ids == 2 * (owner % 4) + t, hp_rows, 0.0), axis=0, keepdims=True
        )
        mz[4 * t : 4 * t + 1, :] = soft / denominator - hot
        mz[4 * t + 1 : 4 * t + 2, :] = jnp.where(low, mix, hp)

    got = [send(mz, az.at[pl.ds(pl.multiple_of(8 * z, 8), 8)], peer(dz=d)) for d in range(1, NZ)]
    az[pl.ds(pl.multiple_of(8 * z, 8), 8), :] = mz[...]
    for copy in got:
        copy.wait_recv()
    for k in range(2):
        my[k * n : (k + 1) * n, :] = az[pl.ds(k, n, stride=per), :]

    got = [send(my, ay.at[y], peer(dy=d)) for d in range(1, NY)]
    ay[y] = my[...]
    for copy in got:
        copy.wait_recv()
    grads = jnp.concatenate([ay[d, 0:n] for d in range(NY)], axis=0)
    feats = jnp.concatenate([ay[d, n : 2 * n] for d in range(NY)], axis=0)
    factor = (rows * NX * NC) ** -0.5
    grads = grads * (id_cols[1].astype(F32) * factor)
    lhs = jnp.concatenate(
        [jnp.where(id_cols[2] == e, feats, 0.0) for e in range(EXAMPLES)], axis=1
    )
    outer = lax.dot_general(
        lhs, grads, TN, precision=lax.Precision.HIGHEST, preferred_element_type=F32
    )
    for e in range(EXAMPLES):
        feat[64 * e : 64 * e + 64, :] = jnp.where(
            low, outer[128 * e + 64 : 128 * e + 128], outer[128 * e : 128 * e + 64]
        )

    span = feat.shape[0] // (NX * NC)
    got = [
        send(
            feat.at[pl.ds(pl.multiple_of(peer(dx, dc)[0] * span, 8), span)],
            rc.at[k], peer(dx, dc),
        )
        for k, (dx, dc) in enumerate(ctx_peers)
    ]
    own = feat[pl.ds(pl.multiple_of(i * span, 8), span), :]
    for copy in got:
        copy.wait_recv()
    mc[...] = own + sum(rc[k] for k in range(len(ctx_peers)))
    got = [send(mc, fa.at[pl.ds(pl.multiple_of(i * span, 8), span)], peer(dx, dc)) for dx, dc in ctx_peers]
    fa[pl.ds(pl.multiple_of(i * span, 8), span), :] = mc[...]
    for copy in got:
        copy.wait_recv()
    m = 32
    for e in range(EXAMPLES):
        even = fa[pl.ds(64 * e, m, stride=2), :]
        odd = fa[pl.ds(64 * e + 1, m, stride=2), :]
        out[0, e] = jnp.where(low, even, pltpu.roll(odd, 64, 1))
        out[1, e] = jnp.where(low, pltpu.roll(even, 64, 1), odd)

    for copy in started:
        copy.wait_send()


def local(
    hidden, head, targets, loss_mask, example_ids, down_input, proj_hidden, proj_vocab, proj_grad,
    proj_act,
):
    rows = hidden.shape[0]
    dm, vc = head.shape
    rank = proj_hidden.shape[1]
    half, quarter = vc // 2, vc // NX
    ids = jnp.stack([targets, loss_mask, example_ids])
    vmem = pl.BlockSpec(memory_space=pltpu.VMEM)
    anywhere = pl.BlockSpec(memory_space=pl.ANY)
    out = pl.pallas_call(
        kernel,
        out_shape=jax.ShapeDtypeStruct((2, EXAMPLES, 32, 128), F32),
        in_specs=[anywhere, anywhere] + [vmem] * 6,
        out_specs=vmem,
        scratch_shapes=[
            pltpu.VMEM((NC, dm, vc), BF16),
            pltpu.VMEM((NX, rows, NC * dm), BF16),
            pltpu.VMEM((2, rows // 2, NC * dm), BF16),
            pltpu.VMEM((NC, rank, dm), BF16),
            pltpu.VMEM((NC, rank, dm), BF16),
            pltpu.VMEM((NX, rank, quarter), F32),
            pltpu.VMEM((NX - 1, rank // NC, quarter), F32),
            pltpu.VMEM((NX, rank, quarter), F32),
            pltpu.VMEM((NX, rows, 128), F32),
            pltpu.VMEM((NX - 1, 8, 128), F32),
            pltpu.VMEM((4, 2, rows, half), F32),
            pltpu.VMEM((2, rows, half), F32),
            pltpu.VMEM((2, 2, rows, half), F32),
            pltpu.VMEM((256, vc), BF16),
            pltpu.VMEM((4 * rows, 128), F32),
            pltpu.VMEM((NY, 4 * rows // NY, 128), F32),
            pltpu.VMEM((8 * NZ, 128), F32),
            pltpu.VMEM((8 * NZ, 128), F32),
            pltpu.VMEM((8, 128), F32),
            pltpu.VMEM((8 * NZ, 128), F32),
            pltpu.VMEM((4 * NZ, 128), F32),
            pltpu.VMEM((NY, 4 * NZ, 128), F32),
            pltpu.VMEM((64 * EXAMPLES, 128), F32),
            pltpu.VMEM((NX * NC - 1, 16, 128), F32),
            pltpu.VMEM((16, 128), F32),
            pltpu.VMEM((64 * EXAMPLES, 128), F32),
            pltpu.SemaphoreType.DMA((2,)),
            pltpu.SemaphoreType.DMA((COPIES,)),
            pltpu.SemaphoreType.DMA((COPIES,)),
        ],
        compiler_params=pltpu.CompilerParams(
            collective_id=0, has_side_effects=True, vmem_limit_bytes=48 * 2**20
        ),
        name="features",
    )(
        hidden, head, ids, down_input.T, proj_hidden.T, proj_vocab.T, proj_grad.T, proj_act.T
    )
    return out[0].reshape(EXAMPLES, rank * rank), out[1].reshape(EXAMPLES, rank * rank)


def solution(mesh):
    return jax.shard_map(
        local,
        mesh=mesh,
        in_specs=(
            P("ctx", None),
            P("ctx", "vocab"),
            P("ctx"),
            P("ctx"),
            P("ctx"),
            P("ctx", "vocab"),
            P("ctx", None),
            P("vocab", None),
            P("ctx", None),
            P("vocab", None),
        ),
        out_specs=(P(), P()),
        check_vma=False,
    )
```

time: 913 us -> 104 us (0.11)
  waiting for transfers between devices: 595 us -> 0 us
  blocking collectives: 264 us -> 0 us
  Pallas kernels: 0 us -> 94.1 us
  matrix products: 20.6 us -> 0 us
  between operations: 14.3 us -> 0.65 us
    psum x3 -> x0, waiting for transfers between devices: 479 us -> none  [the longest x1 267 us: local(): summed = lax.psum(partial_value, ('ctx', 'vocab'))]
    pmax x1 -> x0, blocking collectives: 116 us -> none  [local(): row_top = lax.pmax(local_top, 'vocab')]
    psum x1 -> x0, blocking collectives: 111 us -> none  [local(): row_total = lax.psum(jnp.sum(shifted, axis=1), 'vocab')]
    pallas_call x0 -> x1, Pallas kernels: none -> 94.1 us  [local(): pl.pallas_call(kernel, out_shape=jax.ShapeDtypeStruct((2, EXAMPLES, 32, 1...]
    all_gather x2 -> x0, waiting for transfers between devices: 77.1 us -> none  [the longest x1 77.1 us: local(): every_grad = lax.all_gather(token_grad, 'ctx', axis=0, tiled=True)]
    reduce_scatter x1 -> x0, waiting for transfers between devices: 38.1 us -> none  [local(): lax.psum_scatter(jnp.dot(spread, head, preferred_element_type=jnp.float32...]
    all_to_all x1 -> x0, blocking collectives: 37.7 us -> none  [local(): lax.all_to_all(hidden, 'ctx', split_axis=1, concat_axis=0, tiled=True)]
    dot_general x8 -> x0, matrix products: 20.6 us -> none  [the longest x1 5.86 us: local(): jnp.dot(spread, head, preferred_element_type=jnp.float32)]
  transfers between devices with their start and end apart: 6 -> 0, of which waited for: 5 -> 0; matrix products, arithmetic and copies ran while one was open for 1% -> 0% of each run, Pallas kernels for 0% -> 0%
where the time goes in v1:
time: 104 us
  Pallas kernels  94.1 us (90%)
  local copies, waits for them, and re-layouts  8.31 us (8%)
    pallas_call x1, Pallas kernels, local(): pl.pallas_call(kernel, out_shape=jax.ShapeDtypeStruct((2, EXAMPLES, 32, 1...  94.1 us
    unnamed x15, local copies, waits for them, and re-layouts  7.64 us

profile of v1, /device:TPU:1, one launch (start us, length us, event | category | flops | bytes accessed | tf_op | source)
XLA Modules:
  0.0 103.7 jit_solution(6412898201833491126)
XLA Ops:
  0.6 0.7 pad_add_fusion.ids
  1.3 0.0 copy-start
  1.3 1.6 %copy-done = bf16[128,8192]{1,0:T(8,128)(2,1)S(1)} copy-done((bf16[128,8192]{1,0:T(8,128)(2,1)S(1)}, bf16[128,8192]{1,0:T(8,128)(2,1)}, u32[]{:S(2)}) %copy-start) | copy-done | bytes 2097176
  2.9 0.0 copy-start.1
  2.9 1.6 %copy-done.1 = bf16[1024,1024]{1,0:T(8,128)(2,1)S(1)} copy-done((bf16[1024,1024]{1,0:T(8,128)(2,1)S(1)}, bf16[1024,1024]{1,0:T(8,128)(2,1)}, u32[]{:S(2)}) %copy-start.1) | copy-done | bytes 2097176
  4.5 0.0 copy-start.2
  4.5 0.9 copy-done.2
  5.4 0.0 copy-start.3
  5.4 0.9 copy-done.3
  6.3 0.0 copy-start.4
  6.3 0.9 copy-done.4
  7.2 0.0 copy-start.5
  7.2 0.9 copy-done.5
  8.1 0.0 copy-start.6
  8.1 0.8 copy-done.6
  9.0 94.1 %features.1 = f32[2,2,32,128]{3,2,1,0:T(8,128)S(1)} custom-call(bf16[128,8192]{1,0:T(8,128)(2,1)S(1)} %copy-done, bf16[1024,1024]{1,0:T(8,128)(2,1)S(1)} %copy-done.1, s32[3,128]{1,0:T(4,128)S(1)} %pad_add_fusion.ids, bf16[448,128]{1,0:T(8,128)(2,1)S(1)} %bitcast.21, bf16[64,1024]{1,0:T(8,128)(2,1)S(1)} %bitcast.18, bf16[64,1024]{1,0:T(8,128)(2,1)S(1)} %bitcast.19, ...), custom_call_target="tpu_custom_call" | custom-call | tf_op jit(solution)/shard_map/features/pallas_call | solution.py:326
  103.0 0.7 copy_bitcast_fusion
  (1 shorter events, 0.0 us)
Async XLA Ops:
  1.3 1.6 %copy-start = (bf16[128,8192]{1,0:T(8,128)(2,1)S(1)}, bf16[128,8192]{1,0:T(8,128)(2,1)}, u32[]{:S(2)}) copy-start(bf16[128,8192]{1,0:T(8,128)(2,1)} %hidden.1) | copy-start | bytes 6291460
  2.9 1.6 %copy-start.1 = (bf16[1024,1024]{1,0:T(8,128)(2,1)S(1)}, bf16[1024,1024]{1,0:T(8,128)(2,1)}, u32[]{:S(2)}) copy-start(bf16[1024,1024]{1,0:T(8,128)(2,1)} %head.1) | copy-start | bytes 6291460
  4.5 0.9 copy-start.2
  5.4 0.9 copy-start.3
  6.3 0.9 copy-start.4
  7.2 0.9 copy-start.5
  8.1 0.8 copy-start.6

commit v2 on v1

v2 whole, which is shorter than its diff:
```python
import functools

import jax
import jax.numpy as jnp
from jax import lax
from jax.experimental import pallas as pl
from jax.experimental.pallas import tpu as pltpu
from jax.sharding import PartitionSpec as P

MESH = pl.DeviceIdType.MESH
NX, NC, NY, NZ = 4, 2, 8, 8
EXAMPLES = 2
COPIES = 88
NT = (((1,), (1,)), ((), ()))
TN = (((0,), (0,)), ((), ()))
F32, BF16 = jnp.float32, jnp.bfloat16


def kernel(
    hidden, head, targets, mask, examples, down_input, ph, pv, pg, pa,
    out,
    ids, di, pac, heads, hid, pgs, phs, gpart, grecv, gfull, hps, hrecv,
    part, recv_a, recv_b, w, ve, re, vz, rz, be, vy, ry, vf, rf, my, ay, feat, rc, whole,
    lsem, ssem, rsem,
):
    i, j = lax.axis_index("ctx"), lax.axis_index("vocab")
    x, c = i // NC, i % NC
    z, y = j // NY, j % NY

    def peer(dx=0, dc=0, dy=0, dz=0):
        return (
            ((x + dx) % NX) * NC + (c + dc) % NC,
            ((z + dz) % NZ) * NY + (y + dy) % NY,
        )

    ctx_peers = [(dx, dc) for dx in range(NX) for dc in range(NC) if dx or dc]
    started = []

    def send(src, dst, to):
        k = len(started)
        copy = pltpu.make_async_remote_copy(
            src_ref=src, dst_ref=dst, send_sem=ssem.at[k], recv_sem=rsem.at[k],
            device_id=to, device_id_type=MESH,
        )
        copy.start()
        started.append(copy)
        return copy

    def dot(a, b, dims=NT):
        return lax.dot_general(a, b, dims, preferred_element_type=F32)

    dm = heads.shape[1]
    wide = NC * dm
    vc = heads.shape[2]
    half = vc // 2
    rows = hid.shape[1]
    few = rows // NY
    low = lax.broadcasted_iota(jnp.int32, (1, 128), 1) < 64

    def columns_of(chip):
        return pl.ds(pl.multiple_of(chip * wide, 128), wide)

    loads = [
        pltpu.make_async_copy(src, dst, lsem.at[k])
        for k, (src, dst) in enumerate([
            (head, heads.at[c]),
            (hidden.at[:, columns_of(x)], hid.at[x]),
            (pg, pgs.at[c]),
            (ph, phs.at[c]),
            (pv, w.at[pl.ds(0, 64)]),
            (down_input, di),
            (pa, pac),
            (targets, ids.at[0]),
            (mask, ids.at[1]),
            (examples, ids.at[2]),
        ])
    ]
    for copy in loads:
        copy.start()
    own_head, own_hid, own_pg, own_ph, own_pv, own_di, own_pa = loads[:7]

    barrier = pltpu.get_barrier_semaphore()
    for dx, dc in ctx_peers:
        pl.semaphore_signal(barrier, inc=1, device_id=peer(dx, dc), device_id_type=MESH)
    for d in range(1, NY):
        pl.semaphore_signal(barrier, inc=1, device_id=peer(dy=d), device_id_type=MESH)
    for d in range(1, NZ):
        pl.semaphore_signal(barrier, inc=1, device_id=peer(dz=d), device_id_type=MESH)
    pl.semaphore_wait(barrier, len(ctx_peers) + NY - 1 + NZ - 1)

    right, left = peer(dx=1), peer(dx=NX - 1)
    up, down = peer(dy=1), peer(dy=NY - 1)
    sibling = peer(dc=1)
    xr, xl, xo = (x + 1) % NX, (x + NX - 1) % NX, (x + 2) % NX

    def slab(chip, dy, piece=None):
        at = pl.ds(pl.multiple_of(((y + dy) % NY) * few, few), few)
        if piece is None:
            return hid.at[chip, at]
        return hid.at[chip, at, pl.ds(piece * dm, dm)]

    my_rows = pl.ds(pl.multiple_of(y * few, few), few)
    shares = [
        send(hidden.at[my_rows, columns_of((x + d) % NX)], hid.at[x, my_rows], peer(dx=d))
        for d in (2, 1, 3)
    ]
    blocks = (xo, xl, xr)
    head_copy = send(head, heads.at[c], sibling)
    pg_copy = send(pg, pgs.at[c], sibling)
    ph_copy = send(ph, phs.at[c], sibling)

    def both_ways(arrived, dy, pieces=(None, None)):
        moved = []
        for (from_down, from_up), chip in zip(arrived, blocks):
            from_down.wait_recv()
            going_up = slab(chip, -dy, pieces[0])
            moved_up = send(going_up, going_up, up)
            if from_up is not from_down:
                from_up.wait_recv()
            going_down = slab(chip, dy, pieces[1])
            moved.append((moved_up, send(going_down, going_down, down)))
        return moved

    hops = both_ways([(copy, copy) for copy in shares], 0)

    own_di.wait()
    own_pa.wait()
    act_t = dot(pac[...], di[...], (((1,), (0,)), ((), ())))
    act = jnp.concatenate([act_t, act_t], axis=0).T
    for d in range(NY):
        ve[d, few : 2 * few] = act[d * few : (d + 1) * few]

    own_head.wait()
    own_pg.wait()
    head_copy.wait_recv()
    pg_copy.wait_recv()
    hops = both_ways(hops, 1)
    quarter = vc // NX
    for q in range(NX):
        cols = pl.ds(q * quarter, quarter)
        gpart[q] = sum(
            dot(pgs[k], heads[k, :, cols], (((1,), (0,)), ((), ()))) for k in range(NC)
        )
    share = gpart.shape[1] // NC
    mine = pl.ds(pl.multiple_of(c * share, 8), share)
    g_sum = [
        send(gpart.at[(x + d) % NX, mine], grecv.at[d - 1], peer(dx=d)) for d in range(1, NX)
    ]

    def logits(chip, slot, h):
        cols = pl.ds(h * half, half)
        part[slot, h] = sum(
            dot(
                hid[chip, :, k * dm : (k + 1) * dm], heads[k, :, cols],
                (((1,), (0,)), ((), ())),
            )
            for k in range(NC)
        )

    def project(chip):
        hp = sum(dot(hid[chip, :, k * dm : (k + 1) * dm], phs[k]) for k in range(NC))
        hps[chip] = jnp.concatenate([hp, hp], axis=1)

    own_hid.wait()
    hops = both_ways(hops, 2)
    for h in range(2):
        logits(x, 3, h)
    own_ph.wait()
    ph_copy.wait_recv()
    project(x)

    for copy in g_sum:
        copy.wait_recv()
    gfull[x, mine] = gpart[x, mine] + grecv[0] + grecv[1] + grecv[2]
    g_all = [
        send(gfull.at[x, mine], gfull.at[x, mine], peer(dx=d)) for d in range(1, NX)
    ]
    hops = both_ways(hops, 3, (0, 1))
    for copy in loads[7:]:
        copy.wait()
    id_cols = [jnp.broadcast_to(ids[k], (rows, rows)).T for k in range(3)]
    target = id_cols[0][:, 0:1]
    for copy in g_all:
        copy.wait_recv()
    g_sib = send(gfull.at[:, mine], gfull.at[:, mine], sibling)

    for copies in hops[0]:
        copies.wait_recv()
    logits(xo, 0, 0)
    a_r = send(part.at[0, 0], recv_a.at[0], right)
    logits(xo, 0, 1)
    a_l = send(part.at[0, 1], recv_a.at[1], left)
    for copies in hops[1]:
        copies.wait_recv()
    logits(xl, 2, 0)
    s_l0 = send(part.at[2, 0], recv_b.at[1, 0], left)
    for copies in hops[2]:
        copies.wait_recv()
    logits(xr, 1, 1)
    s_r1 = send(part.at[1, 1], recv_b.at[0, 1], right)
    logits(xl, 2, 1)
    logits(xr, 1, 0)

    own_pv.wait()
    g_sib.wait_recv()
    for q in range(NX):
        cols = pl.ds(q * quarter, quarter)
        g = gfull[q]
        high = g.astype(BF16)
        w[64:128, cols] = high
        w[128:192, cols] = jnp.zeros_like(high)
        w[192:256, cols] = (g - high.astype(F32)).astype(BF16)

    hot = jnp.zeros((rows, 256), F32)
    for h in range(2):
        ids_here = lax.broadcasted_iota(jnp.int32, (rows, half), 1) + (j * vc + h * half)
        onehot = jnp.where(ids_here == target, 1.0, 0.0).astype(BF16)
        hot = hot + dot(onehot, w[:, h * half : (h + 1) * half])
    hot = hot[:, 0:128] + hot[:, 128:256]
    for d in range(NY):
        ve[d, 0:few] = hot[d * few : (d + 1) * few]
    e_sum = [send(ve.at[(y + d) % NY], re.at[d - 1], peer(dy=d)) for d in range(1, NY)]

    a_r.wait_recv()
    part[1, 0] = part[1, 0] + recv_a[0]
    s_r0 = send(part.at[1, 0], recv_b.at[0, 0], right)
    a_l.wait_recv()
    part[2, 1] = part[2, 1] + recv_a[1]
    s_l1 = send(part.at[2, 1], recv_b.at[1, 1], left)

    for chip in blocks:
        project(chip)
    hp_sum = [
        send(hps.at[(x + d) % NX, my_rows], hrecv.at[d - 1], peer(dx=d)) for d in range(1, NX)
    ]

    for copy in e_sum:
        copy.wait_recv()
    vz[...] = ve[y] + sum(re[d] for d in range(NY - 1))
    z_sum = [send(vz, rz.at[z], peer(dz=d)) for d in range(1, NZ)]
    rz[z] = vz[...]
    for copy in hp_sum:
        copy.wait_recv()
    hp = hps[x, my_rows] + hrecv[0] + hrecv[1] + hrecv[2]
    for copy in z_sum:
        copy.wait_recv()
    done = sum(rz[d] for d in range(NZ))
    be[...] = done[0:few]
    my[few : 2 * few] = jnp.where(low, done[few : 2 * few], hp)

    for copy in (s_l0, s_r1, s_r0, s_l1):
        copy.wait_recv()
    vals = [part[3, h] + recv_b[0, h] + recv_b[1, h] for h in range(2)]
    top = jnp.maximum(
        jnp.max(vals[0], axis=1, keepdims=True), jnp.max(vals[1], axis=1, keepdims=True)
    )
    total = jnp.zeros_like(top)
    acc = jnp.zeros((2 * rows, 256), F32)
    for h in range(2):
        e = jnp.exp(vals[h] - top)
        total = total + jnp.sum(e, axis=1, keepdims=True)
        e_high = e.astype(BF16)
        e_low = (e - e_high.astype(F32)).astype(BF16)
        lhs = jnp.concatenate([e_high, e_low], axis=0)
        acc = acc + dot(lhs, w[:, h * half : (h + 1) * half])
    acc = acc[:, 0:128] + acc[:, 128:256]
    soft = acc[0:rows] + acc[rows:]
    stats = jnp.where(low, top, total)
    for d in range(NY):
        at = slice(d * few, (d + 1) * few)
        vy[d, 0:few] = soft[at]
        vy[d, few : 2 * few] = stats[at]

    def combine(parts):
        stats = [p[few : 2 * few] for p in parts]
        tops = [jnp.where(low, s, pltpu.roll(s, 64, 1)) for s in stats]
        best = functools.reduce(jnp.maximum, tops)
        scale = [jnp.exp(t - best) for t in tops]
        value = sum(a * p[0:few] for a, p in zip(scale, parts))
        return value, best, sum(a * s for a, s in zip(scale, stats))

    got = [send(vy.at[(y + d) % NY], ry.at[d - 1], peer(dy=d)) for d in range(1, NY)]
    for copy in got:
        copy.wait_recv()
    value, best, total = combine([vy[y]] + [ry[d] for d in range(NY - 1)])
    vf[0:few] = value
    vf[few : 2 * few] = jnp.where(low, best, total)

    got = [send(vf, rf.at[z], peer(dz=d)) for d in range(1, NZ)]
    rf[z] = vf[...]
    for copy in got:
        copy.wait_recv()
    value, best, total = combine([rf[d] for d in range(NZ)])
    my[0:few] = value / jnp.where(low, pltpu.roll(total, 64, 1), total) - be[...]

    got = [send(my, ay.at[y], peer(dy=d)) for d in range(1, NY)]
    ay[y] = my[...]
    for copy in got:
        copy.wait_recv()
    grads = jnp.concatenate([ay[d, 0:few] for d in range(NY)], axis=0)
    feats = jnp.concatenate([ay[d, few : 2 * few] for d in range(NY)], axis=0)
    factor = (rows * NX * NC) ** -0.5
    grads = grads * (id_cols[1].astype(F32) * factor)
    lhs = jnp.concatenate(
        [jnp.where(id_cols[2] == e, feats, 0.0) for e in range(EXAMPLES)], axis=1
    )
    outer = lax.dot_general(
        lhs, grads, TN, precision=lax.Precision.HIGHEST, preferred_element_type=F32
    )
    for e in range(EXAMPLES):
        feat[64 * e : 64 * e + 64, :] = jnp.where(
            low, outer[128 * e + 64 : 128 * e + 128], outer[128 * e : 128 * e + 64]
        )

    got = [send(feat, rc.at[i], peer(dx, dc)) for dx, dc in ctx_peers]
    rc[i] = feat[...]
    for copy in got:
        copy.wait_recv()
    whole[...] = sum(rc[k] for k in range(NX * NC))
    m = 32
    for e in range(EXAMPLES):
        even = whole[pl.ds(64 * e, m, stride=2), :]
        odd = whole[pl.ds(64 * e + 1, m, stride=2), :]
        out[0, e] = jnp.where(low, even, pltpu.roll(odd, 64, 1))
        out[1, e] = jnp.where(low, pltpu.roll(even, 64, 1), odd)

    for copy in started:
        copy.wait_send()


def local(
    hidden, head, targets, loss_mask, example_ids, down_input, proj_hidden, proj_vocab, proj_grad,
    proj_act,
):
    rows = hidden.shape[0]
    dm, vc = head.shape
    rank = proj_hidden.shape[1]
    half, quarter = vc // 2, vc // NX
    pair = (2 * rows // NY, 128)
    vmem = pl.BlockSpec(memory_space=pltpu.VMEM)
    hbm = pl.BlockSpec(memory_space=pltpu.HBM)
    out = pl.pallas_call(
        kernel,
        out_shape=jax.ShapeDtypeStruct((2, EXAMPLES, 32, 128), F32),
        in_specs=[hbm] * 10,
        out_specs=vmem,
        scratch_shapes=[
            pltpu.VMEM((3, 1, rows), jnp.int32),
            pltpu.VMEM(down_input.shape[::-1], BF16),
            pltpu.VMEM(proj_act.shape[::-1], BF16),
            pltpu.VMEM((NC, dm, vc), BF16),
            pltpu.VMEM((NX, rows, NC * dm), BF16),
            pltpu.VMEM((NC, rank, dm), BF16),
            pltpu.VMEM((NC, rank, dm), BF16),
            pltpu.VMEM((NX, rank, quarter), F32),
            pltpu.VMEM((NX - 1, rank // NC, quarter), F32),
            pltpu.VMEM((NX, rank, quarter), F32),
            pltpu.VMEM((NX, rows, 128), F32),
            pltpu.VMEM((NX - 1, rows // NY, 128), F32),
            pltpu.VMEM((4, 2, rows, half), F32),
            pltpu.VMEM((2, rows, half), F32),
            pltpu.VMEM((2, 2, rows, half), F32),
            pltpu.VMEM((256, vc), BF16),
            pltpu.VMEM((NY,) + pair, F32),
            pltpu.VMEM((NY - 1,) + pair, F32),
            pltpu.VMEM(pair, F32),
            pltpu.VMEM((NZ,) + pair, F32),
            pltpu.VMEM((rows // NY, 128), F32),
            pltpu.VMEM((NY,) + pair, F32),
            pltpu.VMEM((NY - 1,) + pair, F32),
            pltpu.VMEM(pair, F32),
            pltpu.VMEM((NZ,) + pair, F32),
            pltpu.VMEM(pair, F32),
            pltpu.VMEM((NY,) + pair, F32),
            pltpu.VMEM((64 * EXAMPLES, 128), F32),
            pltpu.VMEM((NX * NC, 64 * EXAMPLES, 128), F32),
            pltpu.VMEM((64 * EXAMPLES, 128), F32),
            pltpu.SemaphoreType.DMA((10,)),
            pltpu.SemaphoreType.DMA((COPIES,)),
            pltpu.SemaphoreType.DMA((COPIES,)),
        ],
        compiler_params=pltpu.CompilerParams(
            collective_id=0, has_side_effects=True, vmem_limit_bytes=63 * 2**20
        ),
        name="features",
    )(
        hidden, head, targets.reshape(1, rows), loss_mask.reshape(1, rows),
        example_ids.reshape(1, rows), down_input.T, proj_hidden.T, proj_vocab.T, proj_grad.T,
        proj_act.T,
    )
    return out[0].reshape(EXAMPLES, rank * rank), out[1].reshape(EXAMPLES, rank * rank)


def solution(mesh):
    return jax.shard_map(
        local,
        mesh=mesh,
        in_specs=(
            P("ctx", None),
            P("ctx", "vocab"),
            P("ctx"),
            P("ctx"),
            P("ctx"),
            P("ctx", "vocab"),
            P("ctx", None),
            P("vocab", None),
            P("ctx", None),
            P("vocab", None),
        ),
        out_specs=(P(), P()),
        check_vma=False,
    )
```

time: 104 us -> 81.4 us (0.78)
  Pallas kernels: 94.1 us -> 79.1 us
  local copies, waits for them, and re-layouts: 8.31 us -> 1.46 us
    pallas_call x1, Pallas kernels: 94.1 us -> 79.1 us  [local(): pl.pallas_call(kernel, out_shape=jax.ShapeDtypeStruct((2, EXAMPLES, 32, 1...]
    unnamed x15 -> x1, local copies, waits for them, and re-layouts: 7.64 us -> 0.78 us
where the time goes in v2:
time: 81.4 us; the launch traced here: 81.2 us
  Pallas kernels  79.1 us (97%)
  local copies, waits for them, and re-layouts  1.46 us (2%)
    pallas_call x1, Pallas kernels, local(): pl.pallas_call(kernel, out_shape=jax.ShapeDtypeStruct((2, EXAMPLES, 32, 1...  79.1 us

profile of v2, /device:TPU:1, one launch (start us, length us, event | category | flops | bytes accessed | tf_op | source)
XLA Modules:
  0.0 81.2 jit_solution(17395540547778712096)
XLA Ops:
  0.6 79.1 %features.1 = f32[2,2,32,128]{3,2,1,0:T(8,128)} custom-call(bf16[128,8192]{1,0:T(8,128)(2,1)} %hidden.1, bf16[1024,1024]{1,0:T(8,128)(2,1)} %head.1, s32[1,128]{1,0:T(1,128)} %bitcast.23, s32[1,128]{1,0:T(1,128)} %bitcast.24, s32[1,128]{1,0:T(1,128)} %bitcast.25, bf16[448,128]{1,0:T(8,128)(2,1)} %bitcast.21, bf16[64,1024]{1,0:T(8,128)(2,1)} %bitcast.18, ...), custom_call_target="tpu_custom_call" | custom-call | tf_op jit(solution)/shard_map/features/pallas_call | solution.py:342
  79.7 0.8 slice_bitcast_fusion
  80.5 0.7 copy_bitcast_fusion

commit v3 on v2

v3 whole, which is shorter than its diff:
```python
import functools

import jax
import jax.numpy as jnp
from jax import lax
from jax.experimental import pallas as pl
from jax.experimental.pallas import tpu as pltpu
from jax.sharding import PartitionSpec as P

MESH = pl.DeviceIdType.MESH
NX, NC, NY, NZ = 4, 2, 8, 8
EXAMPLES = 2
COPIES = 86
STEPS = 32767.0
NT = (((1,), (1,)), ((), ()))
TN = (((0,), (0,)), ((), ()))
F32, BF16 = jnp.float32, jnp.bfloat16


def kernel(
    hidden, head, targets, mask, examples, down_input, ph, pv, pg, pa,
    out_head, out_down,
    ids, di, pac, heads, hid, pgs, phs, away, gpart, grecv, gfull, hps, hrecv,
    part, steps, sizes, got_steps, got_sizes, w, ve, re, vz, rz, be, vy, ry, vf, rf, my, ay, ma, aa, feat, rs, mc, rc, whole,
    lsem, ssem, rsem,
):
    i, j = lax.axis_index("ctx"), lax.axis_index("vocab")
    x, c = i // NC, i % NC
    z, y = j // NY, j % NY

    def peer(dx=0, dc=0, dy=0, dz=0):
        return (
            ((x + dx) % NX) * NC + (c + dc) % NC,
            ((z + dz) % NZ) * NY + (y + dy) % NY,
        )

    ctx_peers = [(dx, dc) for dx in range(NX) for dc in range(NC) if dx or dc]
    started = []

    def send(src, dst, to):
        k = len(started)
        copy = pltpu.make_async_remote_copy(
            src_ref=src, dst_ref=dst, send_sem=ssem.at[k], recv_sem=rsem.at[k],
            device_id=to, device_id_type=MESH,
        )
        copy.start()
        started.append(copy)
        return copy

    def dot(a, b, dims=NT):
        return lax.dot_general(a, b, dims, preferred_element_type=F32)

    dm = heads.shape[1]
    wide = NC * dm
    vc = heads.shape[2]
    half = vc // 2
    rows = hid.shape[1]
    few = rows // NY
    low = lax.broadcasted_iota(jnp.int32, (1, 128), 1) < 64

    def columns_of(chip):
        return pl.ds(pl.multiple_of(chip * wide, 128), wide)

    right, left = peer(dx=1), peer(dx=NX - 1)
    up, down = peer(dy=1), peer(dy=NY - 1)
    sibling = peer(dc=1)
    xr, xl, xo = (x + 1) % NX, (x + NX - 1) % NX, (x + 2) % NX

    barrier = pltpu.get_barrier_semaphore()
    greeted = [peer(dx=2), right, left, sibling, up, down]
    greeted += [peer(dz=d) for d in range(1, NZ)]
    for device in greeted:
        pl.semaphore_signal(barrier, inc=1, device_id=device, device_id_type=MESH)

    loads = [
        pltpu.make_async_copy(src, dst, lsem.at[k])
        for k, (src, dst) in enumerate([
            (head, heads.at[c]),
            (hidden.at[:, columns_of(x)], hid.at[x]),
            (hidden.at[:, columns_of(xo)], away.at[0]),
            (hidden.at[:, columns_of(xr)], away.at[1]),
            (hidden.at[:, columns_of(xl)], away.at[2]),
            (pg, pgs.at[c]),
            (ph, phs.at[c]),
            (pv, w.at[pl.ds(0, 64)]),
            (down_input, di),
            (pa, pac),
            (targets, ids.at[0]),
            (mask, ids.at[1]),
            (examples, ids.at[2]),
        ])
    ]
    for copy in loads:
        copy.start()
    own_head, own_hid, *own_away, own_pg, own_ph, own_pv, own_di, own_pa = loads[:10]

    pl.semaphore_wait(barrier, len(greeted))

    def slab(chip, dy, piece=None):
        at = pl.ds(pl.multiple_of(((y + dy) % NY) * few, few), few)
        if piece is None:
            return hid.at[chip, at]
        return hid.at[chip, at, pl.ds(piece * dm, dm)]

    my_rows = pl.ds(pl.multiple_of(y * few, few), few)
    blocks = (xo,)
    for copy in own_away:
        copy.wait()
    shares = [send(away.at[0, my_rows], hid.at[x, my_rows], peer(dx=2))]
    def both_ways(arrived, dy, pieces=(None, None)):
        moved = []
        for (from_down, from_up), chip in zip(arrived, blocks):
            from_down.wait_recv()
            going_up = slab(chip, -dy, pieces[0])
            moved_up = send(going_up, going_up, up)
            if from_up is not from_down:
                from_up.wait_recv()
            going_down = slab(chip, dy, pieces[1])
            moved.append((moved_up, send(going_down, going_down, down)))
        return moved

    hops = both_ways([(copy, copy) for copy in shares], 0)
    hid_r = send(away.at[1], hid.at[x], right)
    hid_l = send(away.at[2], hid.at[x], left)
    own_head.wait()
    head_copy = send(heads.at[c], heads.at[c], sibling)
    own_pg.wait()
    pg_copy = send(pgs.at[c], pgs.at[c], sibling)
    own_ph.wait()
    ph_copy = send(phs.at[c], phs.at[c], sibling)

    own_di.wait()
    own_pa.wait()
    act_t = dot(pac[...], di[...], (((1,), (0,)), ((), ())))
    act = jnp.concatenate([act_t, act_t], axis=0).T
    for d in range(NY):
        ve[d, few : 2 * few] = act[d * few : (d + 1) * few]

    head_copy.wait_recv()
    pg_copy.wait_recv()
    hops = both_ways(hops, 1)
    quarter = vc // NX
    for q in range(NX):
        cols = pl.ds(q * quarter, quarter)
        gpart[q] = sum(
            dot(pgs[k], heads[k, :, cols], (((1,), (0,)), ((), ()))) for k in range(NC)
        )
    share = gpart.shape[1] // NC
    mine = pl.ds(pl.multiple_of(c * share, 8), share)
    g_sum = [
        send(gpart.at[(x + d) % NX, mine], grecv.at[d - 1], peer(dx=d)) for d in range(1, NX)
    ]

    def logits(chip, h):
        cols = pl.ds(h * half, half)
        return sum(
            dot(
                hid[chip, :, k * dm : (k + 1) * dm], heads[k, :, cols],
                (((1,), (0,)), ((), ())),
            )
            for k in range(NC)
        )

    def project(chip):
        hp = sum(dot(hid[chip, :, k * dm : (k + 1) * dm], phs[k]) for k in range(NC))
        hps[chip] = jnp.concatenate([hp, hp], axis=1)

    def pass_on(value, k, to, where):
        largest = jnp.maximum(jnp.max(jnp.abs(value), axis=1, keepdims=True), 1e-30)
        steps[k] = jnp.round(value * (STEPS / largest)).astype(jnp.int32).astype(jnp.int16)
        sizes[k] = jnp.broadcast_to(largest * (1.0 / STEPS), (rows, 128)).T[0:8]
        return (
            send(steps.at[k], got_steps.at[where], to),
            send(sizes.at[k], got_sizes.at[where], to),
        )

    def passed(copies, where):
        for copy in copies:
            copy.wait_recv()
        size = jnp.broadcast_to(got_sizes[where, 0:1], (128, rows)).T[:, 0:1]
        return got_steps[where].astype(jnp.int32).astype(F32) * size

    own_hid.wait()
    hops = both_ways(hops, 2)
    for h in range(2):
        part[0, h] = logits(x, h)
    ph_copy.wait_recv()
    project(x)

    for copy in g_sum:
        copy.wait_recv()
    gfull[x, mine] = gpart[x, mine] + grecv[0] + grecv[1] + grecv[2]
    g_all = [
        send(gfull.at[x, mine], gfull.at[x, mine], peer(dx=d)) for d in range(1, NX)
    ]
    hops = both_ways(hops, 3, (0, 1))
    for copy in loads[10:]:
        copy.wait()
    id_cols = [jnp.broadcast_to(ids[k], (rows, rows)).T for k in range(3)]
    target = id_cols[0][:, 0:1]
    for copy in g_all:
        copy.wait_recv()
    g_sib = send(gfull.at[:, mine], gfull.at[:, mine], sibling)

    for copies in hops[0]:
        copies.wait_recv()
    a_r = pass_on(logits(xo, 0), 0, right, 0)
    a_l = pass_on(logits(xo, 1), 1, left, 1)
    hid_r.wait_recv()
    s_l0 = pass_on(logits(xl, 0), 2, left, 2)
    hid_l.wait_recv()
    s_r1 = pass_on(logits(xr, 1), 3, right, 3)
    part[1, 1] = logits(xl, 1)
    part[1, 0] = logits(xr, 0)

    own_pv.wait()
    g_sib.wait_recv()
    for q in range(NX):
        cols = pl.ds(q * quarter, quarter)
        g = gfull[q]
        high = g.astype(BF16)
        w[64:128, cols] = high
        w[128:192, cols] = jnp.zeros_like(high)
        w[192:256, cols] = (g - high.astype(F32)).astype(BF16)

    hot = jnp.zeros((rows, 256), F32)
    for h in range(2):
        ids_here = lax.broadcasted_iota(jnp.int32, (rows, half), 1) + (j * vc + h * half)
        onehot = jnp.where(ids_here == target, 1.0, 0.0).astype(BF16)
        hot = hot + dot(onehot, w[:, h * half : (h + 1) * half])
    hot = hot[:, 0:128] + hot[:, 128:256]
    for d in range(NY):
        ve[d, 0:few] = hot[d * few : (d + 1) * few]
    e_sum = [send(ve.at[(y + d) % NY], re.at[d - 1], peer(dy=d)) for d in range(1, NY)]

    s_r0 = pass_on(part[1, 0] + passed(a_r, 0), 4, right, 4)
    s_l1 = pass_on(part[1, 1] + passed(a_l, 1), 5, left, 5)
    part[0, 0] = part[0, 0] + passed(s_l0, 2)
    part[0, 1] = part[0, 1] + passed(s_r1, 3)

    for chip in (xl, xr, xo):
        project(chip)
    hp_sum = [
        send(hps.at[(x + d) % NX, my_rows], hrecv.at[d - 1], peer(dx=d)) for d in range(1, NX)
    ]

    for copy in e_sum:
        copy.wait_recv()
    vz[...] = ve[y] + sum(re[d] for d in range(NY - 1))
    z_sum = [send(vz, rz.at[z], peer(dz=d)) for d in range(1, NZ)]
    rz[z] = vz[...]

    vals = [part[0, 0] + passed(s_r0, 4), part[0, 1] + passed(s_l1, 5)]
    top = jnp.maximum(
        jnp.max(vals[0], axis=1, keepdims=True), jnp.max(vals[1], axis=1, keepdims=True)
    )
    total = jnp.zeros_like(top)
    acc = jnp.zeros((2 * rows, 256), F32)
    for h in range(2):
        e = jnp.exp(vals[h] - top)
        total = total + jnp.sum(e, axis=1, keepdims=True)
        e_high = e.astype(BF16)
        e_low = (e - e_high.astype(F32)).astype(BF16)
        lhs = jnp.concatenate([e_high, e_low], axis=0)
        acc = acc + dot(lhs, w[:, h * half : (h + 1) * half])
    acc = acc[:, 0:128] + acc[:, 128:256]
    soft = acc[0:rows] + acc[rows:]
    lane = lax.broadcasted_iota(jnp.int32, (1, 128), 1)
    fold = few // 2

    def pack(top, total):
        first = jnp.where(lane < 32, top[:fold], total[:fold])
        second = jnp.where(lane < 96, top[fold:], total[fold:])
        return jnp.where(low, first, second)

    def unpack(packed, at):
        wide_of = [jnp.broadcast_to(packed[:, at + k : at + k + 1], (fold, 128)) for k in (0, 64)]
        return jnp.concatenate(wide_of, axis=0)

    for d in range(NY):
        at = slice(d * few, (d + 1) * few)
        vy[d, 0:few] = soft[at]
        vy[d, few:] = pack(top[at], total[at])

    def combine(parts):
        tops = [unpack(p[few:], 0) for p in parts]
        best = functools.reduce(jnp.maximum, tops)
        scale = [jnp.exp(t - best) for t in tops]
        value = sum(a * p[0:few] for a, p in zip(scale, parts))
        return value, best, sum(a * unpack(p[few:], 32) for a, p in zip(scale, parts))

    got = [send(vy.at[(y + d) % NY], ry.at[d - 1], peer(dy=d)) for d in range(1, NY)]
    for copy in hp_sum:
        copy.wait_recv()
    hp = hps[x, my_rows] + hrecv[0] + hrecv[1] + hrecv[2]
    for copy in z_sum:
        copy.wait_recv()
    done = sum(rz[d] for d in range(NZ))
    be[...] = done[0:few]
    ma[...] = jnp.where(low, done[few : 2 * few], hp)
    a_all = [send(ma, aa.at[y], peer(dy=d)) for d in range(1, NY)]
    aa[y] = ma[...]
    for copy in got:
        copy.wait_recv()
    value, best, total = combine([vy[y]] + [ry[d] for d in range(NY - 1)])
    vf[0:few] = value
    vf[few:] = pack(best, total)

    got = [send(vf, rf.at[z], peer(dz=d)) for d in range(1, NZ)]
    rf[z] = vf[...]
    for copy in got:
        copy.wait_recv()
    value, best, total = combine([rf[d] for d in range(NZ)])
    my[...] = value / total - be[...]

    got = [send(my, ay.at[y], peer(dy=d)) for d in range(1, NY)]
    ay[y] = my[...]
    for copy in got:
        copy.wait_recv()
    for copy in a_all:
        copy.wait_recv()
    grads = jnp.concatenate([ay[d] for d in range(NY)], axis=0)
    feats = jnp.concatenate([aa[d] for d in range(NY)], axis=0)
    factor = (rows * NX * NC) ** -0.5
    grads = grads * (id_cols[1].astype(F32) * factor)
    lhs = jnp.concatenate(
        [jnp.where(id_cols[2] == e, feats, 0.0) for e in range(EXAMPLES)], axis=1
    )
    outer = lax.dot_general(
        lhs, grads, TN, precision=lax.Precision.HIGHEST, preferred_element_type=F32
    )
    for e in range(EXAMPLES):
        feat[64 * e : 64 * e + 64, :] = jnp.where(
            low, outer[128 * e + 64 : 128 * e + 128], outer[128 * e : 128 * e + 64]
        )

    hf = 32 * EXAMPLES
    other = send(feat.at[pl.ds(pl.multiple_of((1 - c) * hf, 8), hf)], rs, sibling)
    other.wait_recv()
    mc[...] = feat[pl.ds(pl.multiple_of(c * hf, 8), hf), :] + rs[...]
    got = [send(mc, rc.at[x, c], peer(dx, dc)) for dx, dc in ctx_peers]
    rc[x, c] = mc[...]
    for copy in got:
        copy.wait_recv()
    for k in range(NC):
        whole[k * hf : (k + 1) * hf, :] = sum(rc[chip, k] for chip in range(NX))
    m = 32
    for e in range(EXAMPLES):
        even = whole[pl.ds(64 * e, m, stride=2), :]
        odd = whole[pl.ds(64 * e + 1, m, stride=2), :]
        out_head[e] = jnp.where(low, even, pltpu.roll(odd, 64, 1))
        out_down[e] = jnp.where(low, pltpu.roll(even, 64, 1), odd)

    for copy in started:
        copy.wait_send()


def local(
    hidden, head, targets, loss_mask, example_ids, down_input, proj_hidden, proj_vocab, proj_grad,
    proj_act,
):
    rows = hidden.shape[0]
    dm, vc = head.shape
    rank = proj_hidden.shape[1]
    half, quarter = vc // 2, vc // NX
    pair = (2 * rows // NY, 128)
    packed = (3 * rows // (2 * NY), 128)
    vmem = pl.BlockSpec(memory_space=pltpu.VMEM)
    hbm = pl.BlockSpec(memory_space=pltpu.HBM)
    head_features, down_features = pl.pallas_call(
        kernel,
        out_shape=[jax.ShapeDtypeStruct((EXAMPLES, 32, 128), F32)] * 2,
        in_specs=[hbm] * 10,
        out_specs=[vmem] * 2,
        scratch_shapes=[
            pltpu.VMEM((3, 1, rows), jnp.int32),
            pltpu.VMEM(down_input.shape[::-1], BF16),
            pltpu.VMEM(proj_act.shape[::-1], BF16),
            pltpu.VMEM((NC, dm, vc), BF16),
            pltpu.VMEM((NX, rows, NC * dm), BF16),
            pltpu.VMEM((NC, rank, dm), BF16),
            pltpu.VMEM((NC, rank, dm), BF16),
            pltpu.VMEM((NX - 1, rows, NC * dm), BF16),
            pltpu.VMEM((NX, rank, quarter), F32),
            pltpu.VMEM((NX - 1, rank // NC, quarter), F32),
            pltpu.VMEM((NX, rank, quarter), F32),
            pltpu.VMEM((NX, rows, 128), F32),
            pltpu.VMEM((NX - 1, rows // NY, 128), F32),
            pltpu.VMEM((2, 2, rows, half), F32),
            pltpu.VMEM((6, rows, half), jnp.int16),
            pltpu.VMEM((6, 8, 128), F32),
            pltpu.VMEM((6, rows, half), jnp.int16),
            pltpu.VMEM((6, 8, 128), F32),
            pltpu.VMEM((256, vc), BF16),
            pltpu.VMEM((NY,) + pair, F32),
            pltpu.VMEM((NY - 1,) + pair, F32),
            pltpu.VMEM(pair, F32),
            pltpu.VMEM((NZ,) + pair, F32),
            pltpu.VMEM((rows // NY, 128), F32),
            pltpu.VMEM((NY,) + packed, F32),
            pltpu.VMEM((NY - 1,) + packed, F32),
            pltpu.VMEM(packed, F32),
            pltpu.VMEM((NZ,) + packed, F32),
            pltpu.VMEM((rows // NY, 128), F32),
            pltpu.VMEM((NY, rows // NY, 128), F32),
            pltpu.VMEM((rows // NY, 128), F32),
            pltpu.VMEM((NY, rows // NY, 128), F32),
            pltpu.VMEM((64 * EXAMPLES, 128), F32),
            pltpu.VMEM((32 * EXAMPLES, 128), F32),
            pltpu.VMEM((32 * EXAMPLES, 128), F32),
            pltpu.VMEM((NX, NC, 32 * EXAMPLES, 128), F32),
            pltpu.VMEM((64 * EXAMPLES, 128), F32),
            pltpu.SemaphoreType.DMA((13,)),
            pltpu.SemaphoreType.DMA((COPIES,)),
            pltpu.SemaphoreType.DMA((COPIES,)),
        ],
        compiler_params=pltpu.CompilerParams(
            collective_id=0, has_side_effects=True, vmem_limit_bytes=63 * 2**20
        ),
        name="features",
    )(
        hidden, head, targets.reshape(1, rows), loss_mask.reshape(1, rows),
        example_ids.reshape(1, rows), down_input.T, proj_hidden.T, proj_vocab.T, proj_grad.T,
        proj_act.T,
    )
    return tuple(f.reshape(EXAMPLES, rank * rank) for f in (head_features, down_features))


def solution(mesh):
    return jax.shard_map(
        local,
        mesh=mesh,
        in_specs=(
            P("ctx", None),
            P("ctx", "vocab"),
            P("ctx"),
            P("ctx"),
            P("ctx"),
            P("ctx", "vocab"),
            P("ctx", None),
            P("vocab", None),
            P("ctx", None),
            P("vocab", None),
        ),
        out_specs=(P(), P()),
        check_vma=False,
    )
```

time: 81.4 us -> 75.4 us (0.926)
  Pallas kernels: 79.1 us -> 73.1 us
    pallas_call x1, Pallas kernels: 79.1 us -> 73.1 us  [local(): pl.pallas_call(kernel, out_shape=[jax.ShapeDtypeStruct((EXAMPLES, 32, 128...]
    reshape x0 -> x1, local copies, waits for them, and re-layouts: none -> 1.45 us  [local(): f.reshape(EXAMPLES, rank * rank)]
where the time goes in v3:
time: 75.4 us; the launch traced here: 75.2 us
  Pallas kernels  73.1 us (97%)
  local copies, waits for them, and re-layouts  1.45 us (2%)
    pallas_call x1, Pallas kernels, local(): pl.pallas_call(kernel, out_shape=[jax.ShapeDtypeStruct((EXAMPLES, 32, 128...  73.1 us

profile of v3, /device:TPU:1, one launch (start us, length us, event | category | flops | bytes accessed | tf_op | source)
XLA Modules:
  0.0 75.2 jit_solution(275725329070761779)
XLA Ops:
  0.6 73.1 %features.1 = (f32[2,32,128]{2,1,0:T(8,128)}, f32[2,32,128]{2,1,0:T(8,128)}) custom-call(bf16[128,8192]{1,0:T(8,128)(2,1)} %hidden.1, bf16[1024,1024]{1,0:T(8,128)(2,1)} %head.1, s32[1,128]{1,0:T(1,128)} %bitcast.21, s32[1,128]{1,0:T(1,128)} %bitcast.22, s32[1,128]{1,0:T(1,128)} %bitcast.23, bf16[448,128]{1,0:T(8,128)(2,1)} %bitcast.17, ...), custom_call_target="tpu_custom_call" | custom-call | tf_op jit(solution)/shard_map/features/pallas_call | solution.py:370
  73.8 1.5 %copy_bitcast_fusion = (f32[2,4096]{1,0:T(2,128)}, f32[2,4096]{1,0:T(2,128)}) fusion(f32[1,2,32,128]{3,2,1,0:T(8,128)} %bitcast.20, f32[1,2,32,128]{3,2,1,0:T(8,128)} %bitcast.19), kind=kLoop, calls=%fused_computation | loop fusion | bytes 131072 | tf_op jit(solution)/shard_map/reshape | solution.py:426

commit v4 on v3

--- a/solution.py
+++ b/solution.py
@@ -107,6 +107,9 @@
     for copy in own_away:
         copy.wait()
     shares = [send(away.at[0, my_rows], hid.at[x, my_rows], peer(dx=2))]
+    hid_r = send(away.at[1], hid.at[x], right)
+    hid_l = send(away.at[2], hid.at[x], left)
+
     def both_ways(arrived, dy, pieces=(None, None)):
         moved = []
         for (from_down, from_up), chip in zip(arrived, blocks):
@@ -120,8 +123,6 @@
         return moved
 
     hops = both_ways([(copy, copy) for copy in shares], 0)
-    hid_r = send(away.at[1], hid.at[x], right)
-    hid_l = send(away.at[2], hid.at[x], left)
     own_head.wait()
     head_copy = send(heads.at[c], heads.at[c], sibling)
     own_pg.wait()
@@ -213,6 +214,17 @@
     part[1, 1] = logits(xl, 1)
     part[1, 0] = logits(xr, 0)
 
+    s_r0 = pass_on(part[1, 0] + passed(a_r, 0), 4, right, 4)
+    s_l1 = pass_on(part[1, 1] + passed(a_l, 1), 5, left, 5)
+    part[0, 0] = part[0, 0] + passed(s_l0, 2)
+    part[0, 1] = part[0, 1] + passed(s_r1, 3)
+
+    for chip in (xl, xr, xo):
+        project(chip)
+    hp_sum = [
+        send(hps.at[(x + d) % NX, my_rows], hrecv.at[d - 1], peer(dx=d)) for d in range(1, NX)
+    ]
+
     own_pv.wait()
     g_sib.wait_recv()
     for q in range(NX):
@@ -232,23 +244,6 @@
     for d in range(NY):
         ve[d, 0:few] = hot[d * few : (d + 1) * few]
     e_sum = [send(ve.at[(y + d) % NY], re.at[d - 1], peer(dy=d)) for d in range(1, NY)]
-
-    s_r0 = pass_on(part[1, 0] + passed(a_r, 0), 4, right, 4)
-    s_l1 = pass_on(part[1, 1] + passed(a_l, 1), 5, left, 5)
-    part[0, 0] = part[0, 0] + passed(s_l0, 2)
-    part[0, 1] = part[0, 1] + passed(s_r1, 3)
-
-    for chip in (xl, xr, xo):
-        project(chip)
-    hp_sum = [
-        send(hps.at[(x + d) % NX, my_rows], hrecv.at[d - 1], peer(dx=d)) for d in range(1, NX)
-    ]
-
-    for copy in e_sum:
-        copy.wait_recv()
-    vz[...] = ve[y] + sum(re[d] for d in range(NY - 1))
-    z_sum = [send(vz, rz.at[z], peer(dz=d)) for d in range(1, NZ)]
-    rz[z] = vz[...]
 
     vals = [part[0, 0] + passed(s_r0, 4), part[0, 1] + passed(s_l1, 5)]
     top = jnp.maximum(
@@ -290,6 +285,18 @@
         return value, best, sum(a * unpack(p[few:], 32) for a, p in zip(scale, parts))
 
     got = [send(vy.at[(y + d) % NY], ry.at[d - 1], peer(dy=d)) for d in range(1, NY)]
+    for copy in e_sum:
+        copy.wait_recv()
+    vz[...] = ve[y] + sum(re[d] for d in range(NY - 1))
+    z_sum = [send(vz, rz.at[z], peer(dz=d)) for d in range(1, NZ)]
+    rz[z] = vz[...]
+    for copy in got:
+        copy.wait_recv()
+    value, best, total = combine([vy[y]] + [ry[d] for d in range(NY - 1)])
+    vf[0:few] = value
+    vf[few:] = pack(best, total)
+
+    got = [send(vf, rf.at[z], peer(dz=d)) for d in range(1, NZ)]
     for copy in hp_sum:
         copy.wait_recv()
     hp = hps[x, my_rows] + hrecv[0] + hrecv[1] + hrecv[2]
@@ -300,13 +307,6 @@
     ma[...] = jnp.where(low, done[few : 2 * few], hp)
     a_all = [send(ma, aa.at[y], peer(dy=d)) for d in range(1, NY)]
     aa[y] = ma[...]
-    for copy in got:
-        copy.wait_recv()
-    value, best, total = combine([vy[y]] + [ry[d] for d in range(NY - 1)])
-    vf[0:few] = value
-    vf[few:] = pack(best, total)
-
-    got = [send(vf, rf.at[z], peer(dz=d)) for d in range(1, NZ)]
     rf[z] = vf[...]
     for copy in got:
         copy.wait_recv()

time: 75.4 us -> 73.7 us (0.977)
  Pallas kernels: 73.1 us -> 71.4 us
    pallas_call x1, Pallas kernels: 73.1 us -> 71.4 us  [local(): pl.pallas_call(kernel, out_shape=[jax.ShapeDtypeStruct((EXAMPLES, 32, 128...]
where the time goes in v4:
time: 73.7 us; the launch traced here: 73.5 us
  Pallas kernels  71.4 us (97%)
  local copies, waits for them, and re-layouts  1.45 us (2%)
    pallas_call x1, Pallas kernels, local(): pl.pallas_call(kernel, out_shape=[jax.ShapeDtypeStruct((EXAMPLES, 32, 128...  71.4 us

profile of v4, /device:TPU:1, one launch (start us, length us, event | category | flops | bytes accessed | tf_op | source)
XLA Modules:
  0.0 73.5 jit_solution(3256577001682349666)
XLA Ops:
  0.6 71.4 %features.1 = (f32[2,32,128]{2,1,0:T(8,128)}, f32[2,32,128]{2,1,0:T(8,128)}) custom-call(bf16[128,8192]{1,0:T(8,128)(2,1)} %hidden.1, bf16[1024,1024]{1,0:T(8,128)(2,1)} %head.1, s32[1,128]{1,0:T(1,128)} %bitcast.21, s32[1,128]{1,0:T(1,128)} %bitcast.22, s32[1,128]{1,0:T(1,128)} %bitcast.23, bf16[448,128]{1,0:T(8,128)(2,1)} %bitcast.17, ...), custom_call_target="tpu_custom_call" | custom-call | tf_op jit(solution)/shard_map/features/pallas_call | solution.py:370
  72.1 1.5 %copy_bitcast_fusion = (f32[2,4096]{1,0:T(2,128)}, f32[2,4096]{1,0:T(2,128)}) fusion(f32[1,2,32,128]{3,2,1,0:T(8,128)} %bitcast.20, f32[1,2,32,128]{3,2,1,0:T(8,128)} %bitcast.19), kind=kLoop, calls=%fused_computation | loop fusion | bytes 131072 | tf_op jit(solution)/shard_map/reshape | solution.py:426
